TPU v7x, 32 devices: a whole 2x2x4 slice. The times are simulated.
32 devices in a mesh: groups: 2 (over y), dom: 4 (over z), edge: 2 (over x), sub: 2 (over core).
Axes of the slice: x: 2, y: 2, z: 4, core: 2. Of those that a mesh axis runs over, the one named last changes fastest.
Arguments:
- node_lat: bfloat16 [4096, 128], P(('groups', 'dom', 'edge', 'sub')), parts along dimension 0, may hold values from -6 to 6
- edge_lat: bfloat16 [32768, 128], P(('groups', 'dom', 'edge', 'sub')), parts along dimension 0, may hold values from -6 to 6
- node_cot: bfloat16 [4096, 128], P(('groups', 'dom', 'edge', 'sub')), parts along dimension 0, may hold values from -6 to 6
- edge_cot: bfloat16 [32768, 128], P(('groups', 'dom', 'edge', 'sub')), parts along dimension 0, may hold values from -6 to 6
- senders: int32 [32768], P(('groups', 'dom', 'edge', 'sub')), parts along dimension 0, may hold values from 0 to 1023, as said below
- receivers: int32 [32768], P(('groups', 'dom', 'edge', 'sub')), parts along dimension 0, may hold values from 0 to 511
- send_idx: int32 [8, 4, 128], P(('groups', 'dom')), parts along dimension 0, may hold values from 0 to 511, as said below
- send_len: int32 [8, 4], P(('groups', 'dom')), parts along dimension 0, may hold values from 0 to 128, as said below
- edge_count: int32 [8, 4], P(('groups', 'dom'), ('edge', 'sub')), parts along dimension 0, may hold values from 512 to 1024, as said below
- edge_weights: bfloat16 [5, 128, 128], replicated, may hold values from -0.375 to 0.375
- edge_bias: float32 [3, 128], replicated, may hold values from -3 to 3
- edge_gain: float32 [128], replicated, may hold values from 0.1 to 1.9
- edge_shift: float32 [128], replicated, may hold values from -3 to 3
- node_weights: bfloat16 [4, 128, 128], replicated, may hold values from -0.375 to 0.375
- node_bias: float32 [3, 128], replicated, may hold values from -3 to 3
- node_gain: float32 [128], replicated, may hold values from 0.1 to 1.9
Outputs:
- grad_nodes: float32 [4096, 128], P(('groups', 'dom', 'edge', 'sub')), parts along dimension 0
- grad_edges: bfloat16 [32768, 128], P(('groups', 'dom', 'edge', 'sub')), parts along dimension 0
- grad_edge_weights: float32 [10, 128, 128], P('groups'), parts along dimension 0
- grad_edge_vecs: float32 [10, 128], P('groups'), parts along dimension 0
- grad_node_weights: float32 [8, 128, 128], P('groups'), parts along dimension 0
- grad_node_vecs: float32 [8, 128], P('groups'), parts along dimension 0
There are 2 independent parts, one for each index of `groups`. A program takes and returns all parts, laid end to end along the dimension named above; an argument that names none is the same for every part. Nothing has to cross between parts.
Inputs may be any that keep to these rules, and one draw needn't show every extreme that they name: `send_idx`: local node rows of the sending part; entries at or past send_len are not sent. `send_len`: zero where part p + o_k does not exist; some list holds 128 rows in every draw. `senders`: below 512: an own node row of the edge's part; else 512 + k * 128 + j with j below send_len[p - o_k, k]. `edge_count`: every part has a device with all 1024 rows in use.
All inputs are finite; a program needn't handle non-finite values.
Results may differ from a plain program's by a relative error of at most 0.0093.
Values may be sent and summed in bfloat16 or wider, within the bound.
A program may use at most 64 MiB of HBM per device.

v0:
```python
import math

import jax
import jax.numpy as jnp
from jax import lax
from jax.sharding import PartitionSpec as P

EPSILON = 1e-05


def silu_slope(values):
    sigmoid_value = jax.nn.sigmoid(values)
    return sigmoid_value * (1.0 + values * (1.0 - sigmoid_value))


def transposed(left_side, right_side):
    return lax.dot_general(
        left_side, right_side, (((0,), (0,)), ((), ())), preferred_element_type=jnp.float32
    )


def stack_forward(inputs, w_first, w_second, w_third, biases):
    first_pre = jnp.dot(inputs, w_first, preferred_element_type=jnp.float32) + biases[0]
    first_act = jax.nn.silu(first_pre).astype(jnp.bfloat16)
    second_pre = jnp.dot(first_act, w_second, preferred_element_type=jnp.float32) + biases[1]
    second_act = jax.nn.silu(second_pre).astype(jnp.bfloat16)
    third_pre = jnp.dot(second_act, w_third, preferred_element_type=jnp.float32) + biases[2]
    centred = third_pre - jnp.mean(third_pre, axis=1, keepdims=True)
    inv_std = lax.rsqrt(jnp.mean(centred * centred, axis=1, keepdims=True) + EPSILON)
    return (first_pre, first_act, second_pre, second_act, centred * inv_std, inv_std)


def stack_backward(inputs, w_first, w_second, w_third, gains, stored, out_grad):
    first_pre, first_act, second_pre, second_act, normed, inv_std = stored
    scaled = out_grad * gains
    third_grad = inv_std * (
        scaled
        - jnp.mean(scaled, axis=1, keepdims=True)
        - normed * jnp.mean(scaled * normed, axis=1, keepdims=True)
    )
    third_low = third_grad.astype(jnp.bfloat16)
    second_grad = jnp.dot(third_low, w_third.T, preferred_element_type=jnp.float32) * silu_slope(
        second_pre
    )
    second_low = second_grad.astype(jnp.bfloat16)
    first_grad = jnp.dot(second_low, w_second.T, preferred_element_type=jnp.float32) * silu_slope(
        first_pre
    )
    first_low = first_grad.astype(jnp.bfloat16)
    input_grad = jnp.dot(first_low, w_first.T, preferred_element_type=jnp.float32)
    weight_grads = (
        transposed(inputs, first_low),
        transposed(first_act, second_low),
        transposed(second_act, third_low),
    )
    vector_grads = jnp.stack(
        [
            jnp.sum(first_grad, 0),
            jnp.sum(second_grad, 0),
            jnp.sum(third_grad, 0),
            jnp.sum(out_grad * normed, 0),
            jnp.sum(out_grad, 0),
        ]
    )
    return (input_grad, weight_grads, vector_grads)


def local(
    node_lat,
    edge_lat,
    node_cot,
    edge_cot,
    senders,
    receivers,
    send_idx,
    send_len,
    edge_count,
    edge_weights,
    edge_bias,
    edge_gain,
    edge_shift,
    node_weights,
    node_bias,
    node_gain,
):
    features = node_lat.shape[1]
    node_rows = node_lat.shape[0]
    edge_rows = edge_lat.shape[0]
    blocks = send_idx.shape[1]
    reach_parts = blocks // 2
    slot_rows = send_idx.shape[2]
    part_count = lax.axis_size("dom")
    my_part = lax.axis_index("dom")
    inner_count = lax.axis_size(("edge", "sub"))
    part_rows = node_rows * inner_count
    offsets = [
        block_id - reach_parts if block_id < reach_parts else block_id - reach_parts + 1
        for block_id in range(blocks)
    ]
    zero_low = jnp.zeros((), jnp.bfloat16)
    part_table = lax.all_gather(node_lat, ("edge", "sub"), axis=0, tiled=True)
    live_rows = jnp.arange(slot_rows, dtype=jnp.int32)[None, :] < send_len[0][:, None]
    outgoing = jnp.where(live_rows[:, :, None], part_table[send_idx[0]], zero_low)
    packed = jnp.zeros((part_count, slot_rows, features), jnp.bfloat16)
    for block_id in range(blocks):
        target = my_part + offsets[block_id]
        inside = (target >= 0) & (target < part_count)
        packed = packed.at[jnp.clip(target, 0, part_count - 1)].add(
            jnp.where(inside, outgoing[block_id], zero_low)
        )
    received = lax.all_to_all(packed, "dom", split_axis=0, concat_axis=0, tiled=True)
    arrived = []
    for block_id in range(blocks):
        source = my_part - offsets[block_id]
        inside = (source >= 0) & (source < part_count)
        arrived.append(jnp.where(inside, received[jnp.clip(source, 0, part_count - 1)], zero_low))
    extended = jnp.concatenate([part_table] + arrived, axis=0)
    edge_valid = (jnp.arange(edge_rows, dtype=jnp.int32) < edge_count[0, 0])[:, None]
    edge_inputs = jnp.concatenate([edge_lat, extended[senders], extended[receivers]], axis=1)
    edge_first = edge_weights[:3].reshape(3 * features, features)
    edge_stored = stack_forward(
        edge_inputs, edge_first, edge_weights[3], edge_weights[4], edge_bias
    )
    edge_out = jnp.where(edge_valid, edge_stored[4] * edge_gain + edge_shift, 0.0)
    partial_sums = jax.ops.segment_sum(edge_out, receivers, num_segments=part_rows)
    node_first = node_weights[:2].reshape(2 * features, features)
    share_sums = lax.psum_scatter(partial_sums, ("edge", "sub"), scatter_dimension=0, tiled=True)
    node_inputs = jnp.concatenate([node_lat, share_sums.astype(jnp.bfloat16)], axis=1)
    node_stored = stack_forward(
        node_inputs, node_first, node_weights[2], node_weights[3], node_bias
    )
    node_grad, node_wgrads, node_vgrads = stack_backward(
        node_inputs,
        node_first,
        node_weights[2],
        node_weights[3],
        node_gain,
        node_stored,
        node_cot.astype(jnp.float32),
    )
    agg_grad = lax.all_gather(node_grad[:, features:], ("edge", "sub"), axis=0, tiled=True)
    direct_grad = node_cot.astype(jnp.float32) + node_grad[:, :features]
    cot_float = edge_cot.astype(jnp.float32)
    edge_dy = jnp.where(edge_valid, cot_float + agg_grad[receivers], 0.0)
    edge_grad, edge_wgrads, edge_vgrads = stack_backward(
        edge_inputs, edge_first, edge_weights[3], edge_weights[4], edge_gain, edge_stored, edge_dy
    )
    grad_edges = (cot_float + edge_grad[:, :features]).astype(jnp.bfloat16)
    from_senders = jax.ops.segment_sum(
        edge_grad[:, features : 2 * features], senders, num_segments=part_rows + blocks * slot_rows
    )
    owned_grad = from_senders[:part_rows] + jax.ops.segment_sum(
        edge_grad[:, 2 * features :], receivers, num_segments=part_rows
    )
    halo_grad = from_senders[part_rows:].reshape(blocks, slot_rows, features)
    packed_grad = jnp.zeros((part_count, slot_rows, features), jnp.float32)
    for block_id in range(blocks):
        source = my_part - offsets[block_id]
        inside = (source >= 0) & (source < part_count)
        packed_grad = packed_grad.at[jnp.clip(source, 0, part_count - 1)].add(
            jnp.where(inside, halo_grad[block_id], 0.0)
        )
    came_back = lax.all_to_all(
        packed_grad.astype(jnp.bfloat16), "dom", split_axis=0, concat_axis=0, tiled=True
    ).astype(packed_grad.dtype)
    returned = []
    for block_id in range(blocks):
        target = my_part + offsets[block_id]
        inside = (target >= 0) & (target < part_count)
        returned.append(jnp.where(inside, came_back[jnp.clip(target, 0, part_count - 1)], 0.0))
    for block_id in range(blocks):
        owned_grad = owned_grad.at[send_idx[0, block_id]].add(
            jnp.where(live_rows[block_id][:, None], returned[block_id], 0.0)
        )
    node_total = lax.psum_scatter(
        owned_grad.astype(jnp.bfloat16), ("edge", "sub"), scatter_dimension=0, tiled=True
    ).astype(jnp.float32)
    grad_nodes = direct_grad + node_total
    edge_stack = jnp.concatenate(
        [edge_wgrads[0].reshape(3, features, features), edge_wgrads[1][None], edge_wgrads[2][None]],
        axis=0,
    )
    node_stack = jnp.concatenate(
        [node_wgrads[0].reshape(2, features, features), node_wgrads[1][None], node_wgrads[2][None]],
        axis=0,
    )
    totals = lax.psum(
        (edge_stack, edge_vgrads, node_stack, node_vgrads[:4]), ("dom", "edge", "sub")
    )
    edge_scale = 1.0 / math.sqrt(edge_rows * part_count * inner_count)
    node_scale = 1.0 / math.sqrt(node_rows * part_count * inner_count)
    return (
        grad_nodes,
        grad_edges,
        totals[0] * edge_scale,
        totals[1] * edge_scale,
        totals[2] * node_scale,
        totals[3] * node_scale,
    )


def solution(mesh):
    return jax.shard_map(
        local,
        mesh=mesh,
        in_specs=(
            P(("groups", "dom", "edge", "sub"), None),
            P(("groups", "dom", "edge", "sub"), None),
            P(("groups", "dom", "edge", "sub"), None),
            P(("groups", "dom", "edge", "sub"), None),
            P(("groups", "dom", "edge", "sub")),
            P(("groups", "dom", "edge", "sub")),
            P(("groups", "dom"), None, None),
            P(("groups", "dom"), None),
            P(("groups", "dom"), ("edge", "sub")),
            P(),
            P(),
            P(),
            P(),
            P(),
            P(),
            P(),
        ),
        out_specs=(
            P(("groups", "dom", "edge", "sub"), None),
            P(("groups", "dom", "edge", "sub"), None),
            P("groups", None, None),
            P("groups", None),
            P("groups", None, None),
            P("groups", None),
        ),
        check_vma=False,
    )
```

profile of v0, /device:TPU:0, one launch (start us, length us, event | category | flops | bytes accessed | tf_op | source)
XLA Modules:
  0.0 255.0 jit_solution(15522057094794526943)
XLA Ops:
  8.7 6.7 %all_gather.6 = bf16[512,128]{1,0:T(8,128)(2,1)S(1)} all-gather(bf16[128,128]{1,0:T(8,128)(2,1)} %param.32), channel_id=1, replica_groups=mesh['groups'=2,'dom'=4,'edge'=2,'sub'=2] {'edge','sub'}, dimensions={0}, use_global_device_ids=true | all-gather | bytes 163840 | tf_op jit(solution)/shard_map/all_gather | solution.py:101
  19.7 2.0 fusion.47
  21.7 2.0 fusion.48
  23.7 2.0 fusion.49
  25.8 5.3 %all-to-all-start = ((bf16[4,128,128]{2,1,0:T(8,128)(2,1)}), bf16[4,128,128]{2,1,0:T(8,128)(2,1)S(1)}, u32[]{:S(2)}, u32[]{:S(2)}) async-start(bf16[4,128,128]{2,1,0:T(8,128)(2,1)} %fusion.49), calls=%async_computation | async-start | bytes 262144 | tf_op jit(solution)/shard_map/all_to_all | solution.py:111
  31.9 5.6 %all-to-all-done = bf16[4,128,128]{2,1,0:T(8,128)(2,1)S(1)} async-done(((bf16[4,128,128]{2,1,0:T(8,128)(2,1)}), bf16[4,128,128]{2,1,0:T(8,128)(2,1)S(1)}, u32[]{:S(2)}, u32[]{:S(2)}) %all-to-all-start) | async-done | bytes 131104 | tf_op jit(solution)/shard_map/all_to_all | solution.py:111
  37.6 3.2 %gather_fusion.2 = bf16[1024,128]{1,0:T(8,128)(2,1)S(1)} fusion(bf16[1024,128]{1,0:T(8,128)(2,1)S(1)} %bitcast_dynamic-update-slice_fusion, s32[1024]{0:T(1024)S(1)} %get-tuple-element.143), kind=kCustom, calls=%fused_computation.2 | custom fusion | bytes 528384 | tf_op jit(solution)/shard_map/gather | solution.py:119
  40.8 3.2 %gather_fusion.1 = bf16[1024,128]{1,0:T(8,128)(2,1)S(1)} fusion(bf16[1024,128]{1,0:T(8,128)(2,1)S(1)} %bitcast_dynamic-update-slice_fusion, s32[1024]{0:T(1024)S(1)} %get-tuple-element.172), kind=kCustom, calls=%fused_computation.1 | custom fusion | bytes 528384 | tf_op jit(solution)/shard_map/gather | solution.py:119
  46.2 6.7 %scatter_custom_fusion = f32[512,128]{1,0:T(8,128)} fusion(s32[1024]{0:T(1024)S(1)} %copy-done.11, f32[1024,128]{1,0:T(8,128)S(1)} %copy.46, f32[]{:T(128)} %constant.217.clone.1), kind=kCustom, calls=%fused_computation.57 | custom fusion | flops 131072 | bytes 262148 | tf_op jit(solution)/shard_map/scatter-add | solution.py:125
  53.3 19.0 %reduce-scatter.5.cloned.1.call-done = f32[128,128]{1,0:T(8,128)} async-done(((f32[512,128]{1,0:T(8,128)}), f32[128,128]{1,0:T(8,128)}) %reduce-scatter.5.cloned.1.call-update) | async-done | bytes 65552 | tf_op jit(solution)/shard_map/reduce_scatter | solution.py:127
  75.2 5.8 %all_gather.7 = f32[512,128]{1,0:T(8,128)S(1)} all-gather(f32[128,128]{1,0:T(8,128)S(1)} %get-tuple-element.139), channel_id=1, replica_groups=mesh['groups'=2,'dom'=4,'edge'=2,'sub'=2] {'edge','sub'}, dimensions={0}, use_global_device_ids=true | all-gather | bytes 327680 | tf_op jit(solution)/shard_map/all_gather | solution.py:141
  80.9 2.8 %gather_fusion.3 = f32[1024,128]{1,0:T(8,128)S(1)} fusion(f32[512,128]{1,0:T(8,128)S(1)} %all_gather.7, s32[1024]{0:T(1024)S(1)} %get-tuple-element.142), kind=kCustom, calls=%fused_computation.3 | custom fusion | bytes 1052672 | tf_op jit(solution)/shard_map/gather | solution.py:144
  85.3 1.7 fusion.110
  87.4 1.6 fusion.109
  89.8 6.2 %scatter_custom_fusion.1 = f32[1024,128]{1,0:T(8,128)S(1)} fusion(s32[1024]{0:T(1024)S(1)} %copy-done.10, f32[1024,384]{1,0:T(8,128)S(1)} %fusion.9, f32[]{:T(128)} %constant.217.clone.1), kind=kCustom, calls=%fused_computation.31 | custom fusion | flops 131072 | bytes 1048580 | tf_op jit(solution)/shard_map/scatter-add | solution.py:149
  101.0 6.4 %scatter_custom_fusion.2 = f32[512,128]{1,0:T(8,128)S(1)} fusion(f32[512,128]{1,0:T(8,128)S(1)} %slice.316, s32[1024]{0:T(1024)S(1)} %copy-done.11, f32[1024,384]{1,0:T(8,128)S(1)} %fusion.9), kind=kCustom, calls=%fused_computation.29 | custom fusion | flops 131072 | bytes 786432 | tf_op jit(solution)/shard_map/scatter-add | solution.py:152
  107.6 4.6 %all-to-all-start.1 = ((bf16[4,128,128]{2,1,0:T(8,128)(2,1)}), bf16[4,128,128]{2,1,0:T(8,128)(2,1)S(1)}, u32[]{:S(2)}, u32[]{:S(2)}) async-start(bf16[4,128,128]{2,1,0:T(8,128)(2,1)} %convert_element_type.68), calls=%async_computation.2 | async-start | bytes 262144 | tf_op jit(solution)/shard_map/all_to_all | solution.py:163
  113.2 6.4 %all-to-all-done.1 = bf16[4,128,128]{2,1,0:T(8,128)(2,1)S(1)} async-done(((bf16[4,128,128]{2,1,0:T(8,128)(2,1)}), bf16[4,128,128]{2,1,0:T(8,128)(2,1)S(1)}, u32[]{:S(2)}, u32[]{:S(2)}) %all-to-all-start.1) | async-done | bytes 131104 | tf_op jit(solution)/shard_map/all_to_all | solution.py:163
  119.5 1.5 scatter_custom_fusion.3
  126.1 65.9 %all-reduce.4.cloned.1.call-done = (f32[5,128,128]{2,1,0:T(8,128)}, f32[4,128,128]{2,1,0:T(8,128)}) async-done(((f32[5,128,128]{2,1,0:T(8,128)}, f32[4,128,128]{2,1,0:T(8,128)}), (f32[5,128,128]{2,1,0:T(8,128)}, f32[4,128,128]{2,1,0:T(8,128)})) %all-reduce.4.cloned.1.call-update) | async-done | bytes 589840 | tf_op jit(solution)/shard_map/psum | solution.py:187
  192.0 1.7 broadcast_multiply_fusion.1
  193.7 1.7 broadcast_multiply_fusion
  195.4 17.8 %reduce-scatter.7.cloned.1.call-done = bf16[128,128]{1,0:T(8,128)(2,1)} async-done(((bf16[512,128]{1,0:T(8,128)(2,1)}), bf16[128,128]{1,0:T(8,128)(2,1)}) %reduce-scatter.7.cloned.1.call-update) | async-done | bytes 32784
  214.3 32.3 %all-reduce = (f32[5,128]{1,0:T(8,128)S(1)}, f32[4,128]{1,0:T(4,128)S(1)}) all-reduce(f32[5,128]{1,0:T(8,128)S(1)} %stack.38, f32[4,128]{1,0:T(4,128)S(1)} %pad_maximum_fusion.5), channel_id=1, replica_groups=mesh['groups'=2,'dom'=4,'edge'=2,'sub'=2] {'dom','edge','sub'}, use_global_device_ids=true, to_apply=%region_27.28 | all-reduce | flops 1152 | bytes 9216 | tf_op jit(solution)/shard_map/psum | solution.py:187
  (134 shorter events, 27.9 us)
Async XLA Ops:
  7.2 9.7 %copy-start.16 = (s32[3]{0:T(128)S(1)}, s32[3]{0:T(128)}, u32[]{:S(2)}) copy-start(s32[3]{0:T(128)} %constant.227.clone.1) | copy-start | bytes 40
  7.2 24.5 %copy-start.5 = (bf16[5,128,128]{2,1,0:T(8,128)(2,1)S(1)}, bf16[5,128,128]{2,1,0:T(8,128)(2,1)}, u32[]{:S(2)}) copy-start(bf16[5,128,128]{2,1,0:T(8,128)(2,1)} %param.41) | copy-start | bytes 491524
  7.2 24.5 %copy-start.3 = (bf16[1024,128]{1,0:T(8,128)(2,1)S(1)}, bf16[1024,128]{1,0:T(8,128)(2,1)}, u32[]{:S(2)}) copy-start(bf16[1024,128]{1,0:T(8,128)(2,1)} %param.33) | copy-start | bytes 786436
  15.4 16.4 %copy-start.10 = (s32[1024]{0:T(1024)S(1)}, s32[1024]{0:T(1024)}, u32[]{:S(2)}) copy-start(s32[1024]{0:T(1024)} %param.36) | copy-start | bytes 12292
  15.4 16.4 %copy-start.11 = (s32[1024]{0:T(1024)S(1)}, s32[1024]{0:T(1024)}, u32[]{:S(2)}) copy-start(s32[1024]{0:T(1024)} %param.37) | copy-start | bytes 12292
  15.4 16.5 %copy-start.13 = (f32[3,128]{1,0:T(4,128)S(1)}, f32[3,128]{1,0:T(4,128)}, u32[]{:S(2)}) copy-start(f32[3,128]{1,0:T(4,128)} %param.42) | copy-start | bytes 4612
  25.8 11.7 %all-to-all-start = ((bf16[4,128,128]{2,1,0:T(8,128)(2,1)}), bf16[4,128,128]{2,1,0:T(8,128)(2,1)S(1)}, u32[]{:S(2)}, u32[]{:S(2)}) async-start(bf16[4,128,128]{2,1,0:T(8,128)(2,1)} %fusion.49), calls=%async_computation | async-start | bytes 262144 | tf_op jit(solution)/shard_map/all_to_all | solution.py:111
  31.0 41.3 %reduce-scatter.5.cloned.1.call-start = ((), (), s32[]{:S(2)}) async-start(), calls=%async_computation.4 | async-start | bytes 327680 | tf_op jit(solution)/shard_map/reduce_scatter | solution.py:127
  44.8 0.9 copy-start.9
  44.8 0.9 copy-start.15
  45.6 7.4 %copy-start.7 = (bf16[128,128]{1,0:T(8,128)(2,1)S(1)}, bf16[128,128]{1,0:T(8,128)(2,1)}, u32[]{:S(2)}) copy-start(bf16[128,128]{1,0:T(8,128)(2,1)} %param.34) | copy-start | bytes 98308
  45.6 7.5 %copy-start.6 = (bf16[4,128,128]{2,1,0:T(8,128)(2,1)S(1)}, bf16[4,128,128]{2,1,0:T(8,128)(2,1)}, u32[]{:S(2)}) copy-start(bf16[4,128,128]{2,1,0:T(8,128)(2,1)} %param.45) | copy-start | bytes 393220
  45.6 7.5 %copy-start.4 = (bf16[1024,128]{1,0:T(8,128)(2,1)S(1)}, bf16[1024,128]{1,0:T(8,128)(2,1)}, u32[]{:S(2)}) copy-start(bf16[1024,128]{1,0:T(8,128)(2,1)} %param.35) | copy-start | bytes 786436
  45.7 7.6 %copy-start.14 = (f32[3,128]{1,0:T(4,128)S(1)}, f32[3,128]{1,0:T(4,128)}, u32[]{:S(2)}) copy-start(f32[3,128]{1,0:T(4,128)} %param.46) | copy-start | bytes 4612
  45.7 7.6 %copy-start.8 = (s32[1,4,128]{2,1,0:T(4,128)S(1)}, s32[1,4,128]{2,1,0:T(4,128)}, u32[]{:S(2)}) copy-start(s32[1,4,128]{2,1,0:T(4,128)} %param.38) | copy-start | bytes 6148
  45.7 27.4 %copy-start.2 = (bf16[128,128]{1,0:T(8,128)(2,1)S(1)}, bf16[128,128]{1,0:T(8,128)(2,1)}, u32[]{:S(2)}) copy-start(bf16[128,128]{1,0:T(8,128)(2,1)} %param.32) | copy-start | bytes 98308
  46.0 27.8 %copy-start.12 = (f32[128]{0:T(128)S(1)}, f32[128]{0:T(128)}, u32[]{:S(2)}) copy-start(f32[128]{0:T(128)} %param.47) | copy-start | bytes 1540
  52.9 139.1 %all-reduce.4.cloned.1.call-start = ((), (), s32[]{:S(2)}) async-start(), calls=%async_computation.6 | async-start | bytes 1179648 | tf_op jit(solution)/shard_map/psum | solution.py:187
  84.0 1.0 copy-start.20
  85.3 1.7 copy-start.1
  107.4 5.8 %copy-start.17 = (f32[128]{0:T(128)S(1)}, f32[128]{0:T(128)}, u32[]{:S(2)}) copy-start(f32[128]{0:T(128)} %get-tuple-element.166) | copy-start | bytes 1540
  107.4 5.8 %copy-start.18 = (f32[128]{0:T(128)S(1)}, f32[128]{0:T(128)}, u32[]{:S(2)}) copy-start(f32[128]{0:T(128)} %get-tuple-element.164) | copy-start | bytes 1540
  107.6 11.9 %all-to-all-start.1 = ((bf16[4,128,128]{2,1,0:T(8,128)(2,1)}), bf16[4,128,128]{2,1,0:T(8,128)(2,1)S(1)}, u32[]{:S(2)}, u32[]{:S(2)}) async-start(bf16[4,128,128]{2,1,0:T(8,128)(2,1)} %convert_element_type.68), calls=%async_computation.2 | async-start | bytes 262144 | tf_op jit(solution)/shard_map/all_to_all | solution.py:163
  112.2 101.0 %reduce-scatter.7.cloned.1.call-start = ((), (), s32[]{:S(2)}) async-start(), calls=%async_computation.5 | async-start | bytes 163840
  (2 other events, 1.6 us)
Sparse Core Ops, SparseCore 0:
  53.0 19.2 reduce-scatter.4
  99.6 92.3 all-reduce.3
  194.6 18.5 reduce-scatter.6
where the time goes:
time: 256 us; the launch traced here: 255 us
  waiting for transfers between devices  115 us (45%)
  other arithmetic  47.1 us (18%)
  blocking collectives  44.7 us (17%)
  local copies, waits for them, and re-layouts  15.9 us (6%)
  between operations  15.1 us (6%)
  starting transfers between devices  9.94 us (4%)
  matrix products  7.45 us (3%)
    psum x1, waiting for transfers between devices, local(): lax.psum((edge_stack, edge_vgrads, node_stack, node_vgrads[:4]), ('dom',...  65.9 us
    psum x1, blocking collectives, local(): lax.psum((edge_stack, edge_vgrads, node_stack, node_vgrads[:4]), ('dom',...  32.3 us
    reduce_scatter x1, waiting for transfers between devices, local(): lax.psum_scatter(partial_sums, ('edge', 'sub'), scatter_dimension=0, tile...  19 us
    unnamed x4, waiting for transfers between devices  17.8 us
    scatter-add x4, other arithmetic, local(): packed.at[jnp.clip(target, 0, part_count - 1)]  7.39 us
    scatter-add x1, other arithmetic, local(): jax.ops.segment_sum(edge_out, receivers, num_segments=part_rows)  6.69 us
    all_gather x1, blocking collectives, local(): part_table = lax.all_gather(node_lat, ('edge', 'sub'), axis=0, tiled=True)  6.68 us
    all_to_all x1, waiting for transfers between devices, local(): lax.all_to_all(packed_grad.astype(jnp.bfloat16), 'dom', split_axis=0, con...  6.36 us
  transfers between devices with their start and end apart: 5, of which 5 were waited for; matrix products, arithmetic and copies ran while one was open for 8% of the time, Pallas kernels for 0%

commit v1 on v0

v1 whole, which is shorter than its diff:
```python
import functools
import math

import jax
import jax.numpy as jnp
from jax import lax
from jax.experimental import pallas as pl
from jax.experimental.pallas import tpu as pltpu
from jax.sharding import PartitionSpec as P

EPSILON = 1e-05
F32 = jnp.float32
BF16 = jnp.bfloat16
LANES = 128
CHUNK = 256


def nn(left, right):
    return lax.dot_general(left, right, (((1,), (0,)), ((), ())), preferred_element_type=F32)


def nt(left, right):
    return lax.dot_general(left, right, (((1,), (1,)), ((), ())), preferred_element_type=F32)


def tn(left, right):
    return lax.dot_general(left, right, (((0,), (0,)), ((), ())), preferred_element_type=F32)


def sigmoid(values):
    return 0.5 * jnp.tanh(0.5 * values) + 0.5


def slope_of(values):
    gate = sigmoid(values)
    return gate * (1.0 + values * (1.0 - gate))


def silu(values):
    return values * sigmoid(values)


def normalise(pre):
    centred = pre - jnp.mean(pre, axis=1, keepdims=True)
    inv_std = lax.rsqrt(jnp.mean(centred * centred, axis=1, keepdims=True) + EPSILON)
    return centred * inv_std, inv_std


def norm_backward(scaled, normed, inv_std):
    return inv_std * (
        scaled
        - jnp.mean(scaled, axis=1, keepdims=True)
        - normed * jnp.mean(scaled * normed, axis=1, keepdims=True)
    )


def column_sum(values):
    return jnp.sum(values, axis=0, keepdims=True)


def kernel(
    sizes,
    node_lat,
    edge_lat,
    node_cot,
    edge_cot,
    senders,
    receivers,
    send_idx,
    send_len,
    edge_count,
    edge_w,
    edge_b,
    edge_g,
    edge_s,
    node_w,
    node_b,
    node_g,
    out_nodes,
    out_edges,
    out_ew,
    out_ev,
    out_nw,
    out_nv,
    ext,
    outgoing,
    oh_s,
    oht_s,
    oh_r,
    oht_r,
    oh_i,
    proj,
    z1,
    z2,
    a1,
    a2,
    normed_e,
    inv_e,
    low_y,
    sum_send,
    sum_recv,
    agg,
    agg_own,
    d1,
    d2,
    d3,
    back_send,
    back_recv,
    own_acc,
    own_send,
    own_recv,
    nw_stage,
    nw_recv,
    nw_zown,
    nw_z,
    nw_fown,
    nw_full,
    ew_stage,
    ew_recv,
    ew_zown,
    ew_z,
    ew_fown,
    ew_full,
    vec,
    vec_in,
    vec_zown,
    vec_z,
    ag_s,
    ag_r,
    halo_s,
    halo_r,
    sum_s,
    sum_r,
    agg_s,
    agg_r,
    back_s,
    back_r,
    own_s,
    own_r,
    nrs_s,
    nrs_r,
    nz_s,
    nz_r,
    nag_s,
    nag_r,
    ers_s,
    ers_r,
    ez_s,
    ez_r,
    eag_s,
    eag_r,
    vrs_s,
    vrs_r,
    vz_s,
    vz_r,
):
    dom, n_edge, n_sub = sizes
    inner = n_edge * n_sub
    rows = node_lat.shape[0]
    edges = edge_lat.shape[0]
    part_rows = rows * inner
    blocks, slot = send_idx.shape
    ext_rows = part_rows + blocks * slot
    reach = blocks // 2
    offsets = [b - reach if b < reach else b - reach + 1 for b in range(blocks)]
    my_dom = lax.axis_index("dom")
    me = lax.axis_index("edge") * n_sub + lax.axis_index("sub")
    width = LANES // inner
    pending = []

    def inner_id(position):
        return {"edge": position // n_sub, "sub": position % n_sub}

    def remote(src, dst, send, recv, where):
        return pltpu.make_async_remote_copy(
            src_ref=src,
            dst_ref=dst,
            send_sem=send,
            recv_sem=recv,
            device_id=where,
            device_id_type=pl.DeviceIdType.MESH,
        )

    def inner_start(pick_src, pick_dst, send, recv):
        copies = []
        for o in range(1, inner):
            target = (me + o) % inner
            copy = remote(
                pick_src(target, o), pick_dst(me, o), send.at[o], recv.at[o], inner_id(target)
            )
            copy.start()
            copies.append(copy)
            pending.append(copy)
        return copies

    def dom_start(src, pick_dst, send, recv):
        copies = []
        for o in range(1, dom):
            target = (my_dom + o) % dom
            copy = remote(src, pick_dst(my_dom, o), send.at[o], recv.at[o], {"dom": target})
            copy.start()
            copies.append(copy)
            pending.append(copy)
        return copies

    def arrive(copies):
        for copy in copies:
            copy.wait_recv()

    def part_slice(position):
        return pl.ds(pl.multiple_of(position * rows, rows), rows)

    def wslice(position):
        return pl.ds(pl.multiple_of(position * width, width), width)

    barrier = pltpu.get_barrier_semaphore()
    for o in range(1, inner):
        pl.semaphore_signal(
            barrier,
            inc=1,
            device_id=inner_id((me + o) % inner),
            device_id_type=pl.DeviceIdType.MESH,
        )
    for o in range(1, dom):
        pl.semaphore_signal(
            barrier,
            inc=1,
            device_id={"dom": (my_dom + o) % dom},
            device_id_type=pl.DeviceIdType.MESH,
        )
    pl.semaphore_wait(barrier, inner - 1 + dom - 1)

    gathered = inner_start(
        lambda target, o: node_lat, lambda mine, o: ext.at[part_slice(mine)], ag_s, ag_r
    )
    ext[part_slice(me), :] = node_lat[...]

    lane = lax.broadcasted_iota(jnp.int32, (LANES, LANES), 1)
    sublane = lax.broadcasted_iota(jnp.int32, (LANES, LANES), 0)

    def columns_of(row):
        return jnp.transpose(jnp.broadcast_to(row, (LANES, LANES)))

    def hot(mask):
        return jnp.where(mask, 1.0, 0.0).astype(BF16)

    for b in range(blocks):
        row = jnp.where(lane[:1] < send_len[0, b], send_idx[b : b + 1, :], -1)
        column = columns_of(row)
        for t in range(0, part_rows, LANES):
            oh_i[b * slot : (b + 1) * slot, t : t + LANES] = hot(column == lane + t)

    for c in range(edges // LANES):
        span = slice(c * LANES, (c + 1) * LANES)
        row_r = receivers[c : c + 1, :]
        column_r = columns_of(row_r)
        for t in range(0, part_rows, LANES):
            oh_r[span, t : t + LANES] = hot(column_r == lane + t)
            oht_r[t : t + LANES, span] = hot(row_r == sublane + t)
        row_s = senders[c : c + 1, :]
        column_s = columns_of(row_s)
        for t in range(0, ext_rows, LANES):
            oh_s[span, t : t + LANES] = hot(column_s == lane + t)
            oht_s[t : t + LANES, span] = hot(row_s == sublane + t)

    arrive(gathered)

    outgoing[...] = nn(oh_i[...], ext[:part_rows, :]).astype(BF16)
    halo = []
    for b in range(blocks):
        target = my_dom + offsets[b]
        source = my_dom - offsets[b]
        has_target = (target >= 0) & (target < dom)
        has_source = (source >= 0) & (source < dom)
        region = ext.at[part_rows + b * slot : part_rows + (b + 1) * slot]
        copy = remote(
            outgoing.at[b * slot : (b + 1) * slot],
            region,
            halo_s.at[b],
            halo_r.at[b],
            {"dom": lax.clamp(0, target, dom - 1)},
        )
        pl.when(has_target)(copy.start)

        @pl.when(jnp.logical_not(has_source))
        def _(region=region):
            region[...] = jnp.zeros(region.shape, BF16)

        halo.append((copy, has_target, has_source))

    proj[part_rows + blocks * slot :, :] = nn(ext[:part_rows, :], edge_w[2]).astype(BF16)
    proj[:part_rows, :] = nn(ext[:part_rows, :], edge_w[1]).astype(BF16)
    for c in range(0, edges, CHUNK):
        span = slice(c, c + CHUNK)
        z1[span, :] = (
            nn(edge_lat[span, :], edge_w[0])
            + nn(oh_r[span, :], proj[ext_rows:, :])
            + nn(oh_s[span, :part_rows], proj[:part_rows, :])
            + edge_b[0:1, :]
        )

    for copy, has_target, has_source in halo:
        pl.when(has_source)(copy.wait_recv)
    proj[part_rows:ext_rows, :] = nn(ext[part_rows:, :], edge_w[1]).astype(BF16)

    for c in range(0, edges, CHUNK):
        span = slice(c, c + CHUNK)
        first = z1[span, :] + nn(oh_s[span, part_rows:], proj[part_rows:ext_rows, :])
        z1[span, :] = first
        act1 = silu(first).astype(BF16)
        a1[span, :] = act1
        second = nn(act1, edge_w[3]) + edge_b[1:2, :]
        z2[span, :] = second
        act2 = silu(second).astype(BF16)
        a2[span, :] = act2
        normed, inv_std = normalise(nn(act2, edge_w[4]) + edge_b[2:3, :])
        normed_e[span, :] = normed
        inv_e[span, :] = inv_std
        valid = lax.broadcasted_iota(jnp.int32, (CHUNK, 1), 0) + c < edge_count[0, 0]
        low_y[span, :] = jnp.where(valid, normed * edge_g[...] + edge_s[...], 0.0).astype(BF16)

    own_acc[...] = nn(oht_r[...], low_y[...])
    sum_send[...] = own_acc[...].astype(BF16)
    summing = inner_start(
        lambda target, o: sum_send.at[part_slice(target)],
        lambda mine, o: sum_recv.at[o],
        sum_s,
        sum_r,
    )

    z1[...] = slope_of(z1[...])
    z2[...] = slope_of(z2[...])
    node_base = nn(node_lat[...], node_w[0]) + node_b[0:1, :]
    cot_n = node_cot[...].astype(F32)

    arrive(summing)
    total = own_acc[part_slice(me), :]
    for o in range(1, inner):
        total = total + sum_recv[o].astype(F32)
    total_low = total.astype(BF16)

    pre1 = node_base + nn(total_low, node_w[1])
    n1 = silu(pre1).astype(BF16)
    pre2 = nn(n1, node_w[2]) + node_b[1:2, :]
    n2 = silu(pre2).astype(BF16)
    normed_n, inv_n = normalise(nn(n2, node_w[3]) + node_b[2:3, :])
    g3 = norm_backward(cot_n * node_g[...], normed_n, inv_n)
    g3_low = g3.astype(BF16)
    g2 = nt(g3_low, node_w[3]) * slope_of(pre2)
    g2_low = g2.astype(BF16)
    g1 = nt(g2_low, node_w[2]) * slope_of(pre1)
    g1_low = g1.astype(BF16)
    agg_own[...] = nt(g1_low, node_w[1]).astype(BF16)
    aggregating = inner_start(
        lambda target, o: agg_own, lambda mine, o: agg.at[part_slice(mine)], agg_s, agg_r
    )
    agg[part_slice(me), :] = agg_own[...]

    out_nodes[...] = cot_n + nt(g1_low, node_w[0])
    nw_stage[0] = tn(node_lat[...], g1_low).astype(BF16)
    nw_stage[1] = tn(total_low, g1_low).astype(BF16)
    nw_stage[2] = tn(n1, g2_low).astype(BF16)
    nw_stage[3] = tn(n2, g3_low).astype(BF16)
    vec[8:9, :] = column_sum(g1)
    vec[9:10, :] = column_sum(g2)
    vec[10:11, :] = column_sum(g3)
    vec[11:12, :] = column_sum(cot_n * normed_n)
    vec[12:16, :] = jnp.zeros((4, LANES), F32)
    vec[5:8, :] = jnp.zeros((3, LANES), F32)

    def reduce_start(stage, recv, send, got):
        return inner_start(
            lambda target, o: stage.at[:, wslice(target), :],
            lambda mine, o: recv.at[o],
            send,
            got,
        )

    def reduce_finish(stage, recv, zown, z, send, got):
        partial = stage[:, wslice(me), :].astype(F32)
        for o in range(1, inner):
            partial = partial + recv[o].astype(F32)
        partial = partial.astype(BF16)
        zown[...] = partial
        z[my_dom] = partial
        return dom_start(zown, lambda mine, o: z.at[mine], send, got)

    def gather_start(z, fown, full, send, got):
        partial = z[0].astype(F32)
        for d in range(1, dom):
            partial = partial + z[d].astype(F32)
        partial = partial.astype(BF16)
        fown[...] = partial
        full[:, wslice(me), :] = partial
        return inner_start(
            lambda target, o: fown, lambda mine, o: full.at[:, wslice(mine), :], send, got
        )

    node_rs = reduce_start(nw_stage, nw_recv, nrs_s, nrs_r)

    arrive(aggregating)
    sums = [jnp.zeros((1, LANES), F32) for _ in range(5)]
    for c in range(0, edges, CHUNK):
        span = slice(c, c + CHUNK)
        valid = lax.broadcasted_iota(jnp.int32, (CHUNK, 1), 0) + c < edge_count[0, 0]
        cot = edge_cot[span, :].astype(F32)
        dy = jnp.where(valid, cot + nn(oh_r[span, :], agg[...]), 0.0)
        normed = normed_e[span, :]
        h3 = norm_backward(dy * edge_g[...], normed, inv_e[span, :])
        h3_low = h3.astype(BF16)
        d3[span, :] = h3_low
        h2 = nt(h3_low, edge_w[4]) * z2[span, :]
        h2_low = h2.astype(BF16)
        d2[span, :] = h2_low
        h1 = nt(h2_low, edge_w[3]) * z1[span, :]
        h1_low = h1.astype(BF16)
        d1[span, :] = h1_low
        out_edges[span, :] = (cot + nt(h1_low, edge_w[0])).astype(BF16)
        for position, term in enumerate((h1, h2, h3, dy * normed, dy)):
            sums[position] = sums[position] + column_sum(term)

    for position in range(5):
        vec[position : position + 1, :] = sums[position]
    vec_in[me] = vec[...]
    vec_rs = inner_start(lambda target, o: vec, lambda mine, o: vec_in.at[mine], vrs_s, vrs_r)

    back_send[...] = nn(oht_s[part_rows:, :], d1[...]).astype(BF16)
    returning = []
    for b in range(blocks):
        target = my_dom - offsets[b]
        source = my_dom + offsets[b]
        has_target = (target >= 0) & (target < dom)
        has_source = (source >= 0) & (source < dom)
        region = back_recv.at[b * slot : (b + 1) * slot]
        copy = remote(
            back_send.at[b * slot : (b + 1) * slot],
            region,
            back_s.at[b],
            back_r.at[b],
            {"dom": lax.clamp(0, target, dom - 1)},
        )
        pl.when(has_target)(copy.start)

        @pl.when(jnp.logical_not(has_source))
        def _(region=region):
            region[...] = jnp.zeros(region.shape, BF16)

        returning.append((copy, has_target, has_source))

    own_low = nn(oht_s[:part_rows, :], d1[...]).astype(BF16)
    recv_low = nn(oht_r[...], d1[...]).astype(BF16)
    ew_stage[0] = tn(edge_lat[...], d1[...]).astype(BF16)
    ew_stage[1] = (tn(ext[:part_rows, :], own_low) + tn(ext[part_rows:, :], back_send[...])).astype(
        BF16
    )
    ew_stage[2] = tn(ext[:part_rows, :], recv_low).astype(BF16)
    ew_stage[3] = tn(a1[...], d2[...]).astype(BF16)
    ew_stage[4] = tn(a2[...], d3[...]).astype(BF16)
    edge_rs = reduce_start(ew_stage, ew_recv, ers_s, ers_r)
    own_acc[...] = nt(own_low, edge_w[1]) + nt(recv_low, edge_w[2])

    arrive(node_rs)
    node_z = reduce_finish(nw_stage, nw_recv, nw_zown, nw_z, nz_s, nz_r)

    for copy, has_target, has_source in returning:
        pl.when(has_source)(copy.wait_recv)
    scattered = tn(oh_i[...], back_recv[...]).astype(BF16)
    own_acc[...] = own_acc[...] + nt(scattered, edge_w[1])
    own_send[...] = own_acc[...].astype(BF16)
    owning = inner_start(
        lambda target, o: own_send.at[part_slice(target)],
        lambda mine, o: own_recv.at[o],
        own_s,
        own_r,
    )

    arrive(edge_rs)
    edge_z = reduce_finish(ew_stage, ew_recv, ew_zown, ew_z, ez_s, ez_r)
    arrive(vec_rs)
    vec_sum = vec_in[0]
    for position in range(1, inner):
        vec_sum = vec_sum + vec_in[position]
    vec_zown[...] = vec_sum
    vec_z[my_dom] = vec_sum
    vec_all = dom_start(vec_zown, lambda mine, o: vec_z.at[mine], vz_s, vz_r)

    arrive(node_z)
    node_ag = gather_start(nw_z, nw_fown, nw_full, nag_s, nag_r)

    arrive(owning)
    mine = own_acc[part_slice(me), :]
    for o in range(1, inner):
        mine = mine + own_recv[o].astype(F32)
    out_nodes[...] = out_nodes[...] + mine

    arrive(edge_z)
    edge_ag = gather_start(ew_z, ew_fown, ew_full, eag_s, eag_r)

    edge_scale = 1.0 / math.sqrt(edges * dom * inner)
    node_scale = 1.0 / math.sqrt(rows * dom * inner)
    arrive(vec_all)
    vec_sum = vec_z[0]
    for d in range(1, dom):
        vec_sum = vec_sum + vec_z[d]
    out_ev[...] = vec_sum[0:5, :] * edge_scale
    out_nv[...] = vec_sum[8:12, :] * node_scale
    arrive(node_ag)
    out_nw[...] = nw_full[...].astype(F32) * node_scale
    arrive(edge_ag)
    out_ew[...] = ew_full[...].astype(F32) * edge_scale

    for copy in pending:
        copy.wait_send()
    for copy, has_target, has_source in halo + returning:
        pl.when(has_target)(copy.wait_send)


def local(sizes, *arrays):
    (
        node_lat,
        edge_lat,
        node_cot,
        edge_cot,
        senders,
        receivers,
        send_idx,
        send_len,
        edge_count,
        edge_w,
        edge_b,
        edge_g,
        edge_s,
        node_w,
        node_b,
        node_g,
    ) = arrays
    dom, n_edge, n_sub = sizes
    inner = n_edge * n_sub
    rows, features = node_lat.shape
    edges = edge_lat.shape[0]
    blocks, slot = send_idx.shape[1:]
    part_rows = rows * inner
    ext_rows = part_rows + blocks * slot
    width = features // inner
    operands = (
        node_lat,
        edge_lat,
        node_cot,
        edge_cot,
        senders.reshape(edges // LANES, LANES),
        receivers.reshape(edges // LANES, LANES),
        send_idx[0],
        send_len,
        edge_count,
        edge_w,
        edge_b,
        edge_g.reshape(1, features),
        edge_s.reshape(1, features),
        node_w,
        node_b,
        node_g.reshape(1, features),
    )
    vmem = pl.BlockSpec(memory_space=pltpu.VMEM)
    smem = pl.BlockSpec(memory_space=pltpu.SMEM)
    in_specs = [smem if position in (7, 8) else vmem for position in range(len(operands))]

    def low(*shape):
        return pltpu.VMEM(shape + (features,), BF16)

    def full(*shape):
        return pltpu.VMEM(shape + (features,), F32)

    def weights(count):
        return [
            low(count, features),
            low(inner, count, width),
            low(count, width),
            low(dom, count, width),
            low(count, width),
            low(count, features),
        ]

    def sems(count):
        return [pltpu.SemaphoreType.DMA((count,)), pltpu.SemaphoreType.DMA((count,))]

    scratch = [
        low(ext_rows),
        low(blocks * slot),
        pltpu.VMEM((edges, ext_rows), BF16),
        pltpu.VMEM((ext_rows, edges), BF16),
        pltpu.VMEM((edges, part_rows), BF16),
        pltpu.VMEM((part_rows, edges), BF16),
        pltpu.VMEM((blocks * slot, part_rows), BF16),
        low(ext_rows + part_rows),
        full(edges),
        full(edges),
        low(edges),
        low(edges),
        full(edges),
        pltpu.VMEM((edges, 1), F32),
        low(edges),
        low(part_rows),
        low(inner, rows),
        low(part_rows),
        low(rows),
        low(edges),
        low(edges),
        low(edges),
        low(blocks * slot),
        low(blocks * slot),
        full(part_rows),
        low(part_rows),
        low(inner, rows),
        *weights(4),
        *weights(5),
        full(16),
        full(inner, 16),
        full(16),
        full(dom, 16),
        *sems(inner),
        *sems(blocks),
        *sems(inner),
        *sems(inner),
        *sems(blocks),
        *sems(inner),
        *sems(inner),
        *sems(dom),
        *sems(inner),
        *sems(inner),
        *sems(dom),
        *sems(inner),
        *sems(inner),
        *sems(dom),
    ]
    return pl.pallas_call(
        functools.partial(kernel, sizes),
        out_shape=(
            jax.ShapeDtypeStruct((rows, features), F32),
            jax.ShapeDtypeStruct((edges, features), BF16),
            jax.ShapeDtypeStruct((5, features, features), F32),
            jax.ShapeDtypeStruct((5, features), F32),
            jax.ShapeDtypeStruct((4, features, features), F32),
            jax.ShapeDtypeStruct((4, features), F32),
        ),
        in_specs=in_specs,
        out_specs=(vmem,) * 6,
        scratch_shapes=scratch,
        compiler_params=pltpu.CompilerParams(
            collective_id=0, has_side_effects=True, vmem_limit_bytes=48 * 1024 * 1024
        ),
    )(*operands)


def solution(mesh):
    sizes = (mesh.shape["dom"], mesh.shape["edge"], mesh.shape["sub"])
    part = P(("groups", "dom", "edge", "sub"), None)
    index = P(("groups", "dom", "edge", "sub"))
    return jax.shard_map(
        functools.partial(local, sizes),
        mesh=mesh,
        in_specs=(
            part,
            part,
            part,
            part,
            index,
            index,
            P(("groups", "dom"), None, None),
            P(("groups", "dom"), None),
            P(("groups", "dom"), ("edge", "sub")),
        )
        + (P(),) * 7,
        out_specs=(
            part,
            part,
            P("groups", None, None),
            P("groups", None),
            P("groups", None, None),
            P("groups", None),
        ),
        check_vma=False,
    )
```

time: 256 us -> 54.1 us (0.21)
  waiting for transfers between devices: 115 us -> 0 us
  other arithmetic: 47.1 us -> 0 us
  blocking collectives: 44.7 us -> 0 us
  Pallas kernels: 0 us -> 40.4 us
  between operations: 15.1 us -> 1.38 us
  starting transfers between devices: 9.94 us -> 0 us
  matrix products: 7.45 us -> 0 us
  local copies, waits for them, and re-layouts: 15.9 us -> 11.8 us
    psum x1 -> x0, waiting for transfers between devices: 65.9 us -> none  [local(): lax.psum((edge_stack, edge_vgrads, node_stack, node_vgrads[:4]), ('dom',...]
    pallas_call x0 -> x1, Pallas kernels: none -> 40.4 us  [local(): pl.pallas_call(functools.partial(kernel, sizes), out_shape=(jax.ShapeDtyp...]
    scatter-add x15 -> x0, other arithmetic: 35.1 us -> none  [the longest x4 7.39 us: local(): packed.at[jnp.clip(target, 0, part_count - 1)]]
    psum x1 -> x0, blocking collectives: 32.3 us -> none  [local(): lax.psum((edge_stack, edge_vgrads, node_stack, node_vgrads[:4]), ('dom',...]
    reduce_scatter x1 -> x0, waiting for transfers between devices: 19 us -> none  [local(): lax.psum_scatter(partial_sums, ('edge', 'sub'), scatter_dimension=0, tile...]
    unnamed x4 -> x0, waiting for transfers between devices: 17.8 us -> none
    all_gather x2 -> x0, blocking collectives: 12.5 us -> none  [the longest x1 6.68 us: local(): part_table = lax.all_gather(node_lat, ('edge', 'sub'), axis=0, tiled=True)]
    all_to_all x2 -> x0, waiting for transfers between devices: 12 us -> none  [the longest x1 6.36 us: local(): lax.all_to_all(packed_grad.astype(jnp.bfloat16), 'dom', split_axis=0, con...]
  transfers between devices with their start and end apart: 5 -> 0, of which waited for: 5 -> 0; matrix products, arithmetic and copies ran while one was open for 8% -> 0% of each run, Pallas kernels for 0% -> 0%
where the time goes in v1:
time: 54.1 us; the launch traced here: 53.6 us
  Pallas kernels  40.4 us (75%)
  local copies, waits for them, and re-layouts  11.8 us (22%)
  between operations  1.38 us (3%)
    pallas_call x1, Pallas kernels, local(): pl.pallas_call(functools.partial(kernel, sizes), out_shape=(jax.ShapeDtyp...  40.4 us
    unnamed x36, local copies, waits for them, and re-layouts  11.8 us

profile of v1, /device:TPU:0, one launch (start us, length us, event | category | flops | bytes accessed | tf_op | source)
XLA Modules:
  0.0 53.6 jit_solution(12286559471860377476)
XLA Ops:
  0.6 0.0 copy-start.9
  1.3 0.0 copy-start.8
  1.3 0.0 copy-start.7
  1.3 0.0 copy-start.6
  1.4 0.6 %copy-done.8 = s32[1,4,128]{2,1,0:T(4,128)S(1)} copy-done((s32[1,4,128]{2,1,0:T(4,128)S(1)}, s32[1,4,128]{2,1,0:T(4,128)}, u32[]{:S(2)}) %copy-start.8) | copy-done | bytes 2072
  2.0 0.0 copy-done.7
  2.0 0.0 copy-done.6
  2.0 0.0 copy-done.12
  2.0 0.9 %copy-done = bf16[1024,128]{1,0:T(8,128)(2,1)S(1)} copy-done((bf16[1024,128]{1,0:T(8,128)(2,1)S(1)}, bf16[1024,128]{1,0:T(8,128)(2,1)}, u32[]{:S(2)}) %copy-start) | copy-done | bytes 262168
  3.0 0.9 %copy-done.1 = bf16[1024,128]{1,0:T(8,128)(2,1)S(1)} copy-done((bf16[1024,128]{1,0:T(8,128)(2,1)S(1)}, bf16[1024,128]{1,0:T(8,128)(2,1)}, u32[]{:S(2)}) %copy-start.1) | copy-done | bytes 262168
  3.9 0.9 %copy-done.2 = bf16[5,128,128]{2,1,0:T(8,128)(2,1)S(1)} copy-done((bf16[5,128,128]{2,1,0:T(8,128)(2,1)S(1)}, bf16[5,128,128]{2,1,0:T(8,128)(2,1)}, u32[]{:S(2)}) %copy-start.2) | copy-done | bytes 163864
  4.9 0.9 %copy-done.3 = bf16[4,128,128]{2,1,0:T(8,128)(2,1)S(1)} copy-done((bf16[4,128,128]{2,1,0:T(8,128)(2,1)S(1)}, bf16[4,128,128]{2,1,0:T(8,128)(2,1)}, u32[]{:S(2)}) %copy-start.3) | copy-done | bytes 131096
  5.8 0.8 %copy-done.4 = bf16[128,128]{1,0:T(8,128)(2,1)S(1)} copy-done((bf16[128,128]{1,0:T(8,128)(2,1)S(1)}, bf16[128,128]{1,0:T(8,128)(2,1)}, u32[]{:S(2)}) %copy-start.4) | copy-done | bytes 32792
  6.5 0.8 %copy-done.5 = bf16[128,128]{1,0:T(8,128)(2,1)S(1)} copy-done((bf16[128,128]{1,0:T(8,128)(2,1)S(1)}, bf16[128,128]{1,0:T(8,128)(2,1)}, u32[]{:S(2)}) %copy-start.5) | copy-done | bytes 32792
  7.3 0.7 %copy-done.10 = f32[3,128]{1,0:T(4,128)S(1)} copy-done((f32[3,128]{1,0:T(4,128)S(1)}, f32[3,128]{1,0:T(4,128)}, u32[]{:S(2)}) %copy-start.10) | copy-done | bytes 1560
  8.0 0.7 %copy-done.13 = f32[128]{0:T(128)S(1)} copy-done((f32[128]{0:T(128)S(1)}, f32[128]{0:T(128)}, u32[]{:S(2)}) %copy-start.13) | copy-done | bytes 536
  8.6 0.7 %copy-done.14 = f32[128]{0:T(128)S(1)} copy-done((f32[128]{0:T(128)S(1)}, f32[128]{0:T(128)}, u32[]{:S(2)}) %copy-start.14) | copy-done | bytes 536
  9.3 40.4 %shard_map.199 = (f32[128,128]{1,0:T(8,128)S(1)}, bf16[1024,128]{1,0:T(8,128)(2,1)S(1)}, f32[5,128,128]{2,1,0:T(8,128)S(1)}, f32[5,128]{1,0:T(8,128)S(1)}, f32[4...) custom-call(bf16[128,128]{1,0:T(8,128)(2,1)S(1)} %copy-done.4, bf16[1024,128]{1,0:T(8,128)(2,1)S(1)} %copy-done, ...), custom_call_target="tpu_custom_call" | custom-call | tf_op jit(solution)/shard_map/pallas_call | solution.py:635
  49.7 0.6 %copy.29 = f32[128,128]{1,0:T(8,128)} copy(f32[128,128]{1,0:T(8,128)S(1)} %get-tuple-element.12) | data formatting | bytes 131072
  50.3 0.7 %copy.30 = bf16[1024,128]{1,0:T(8,128)(2,1)} copy(bf16[1024,128]{1,0:T(8,128)(2,1)S(1)} %get-tuple-element.13) | data formatting | bytes 524288
  51.0 0.7 %copy.31 = f32[5,128,128]{2,1,0:T(8,128)} copy(f32[5,128,128]{2,1,0:T(8,128)S(1)} %get-tuple-element.14) | data formatting | bytes 655360
  51.7 0.6 %copy.32 = f32[5,128]{1,0:T(8,128)} copy(f32[5,128]{1,0:T(8,128)S(1)} %get-tuple-element.15) | data formatting | bytes 5120
  52.3 0.7 %copy.33 = f32[4,128,128]{2,1,0:T(8,128)} copy(f32[4,128,128]{2,1,0:T(8,128)S(1)} %get-tuple-element.16) | data formatting | bytes 524288
  53.0 0.6 %copy.34 = f32[4,128]{1,0:T(4,128)} copy(f32[4,128]{1,0:T(4,128)S(1)} %get-tuple-element.17) | data formatting | bytes 4096
  (13 shorter events, 0.0 us)
Async XLA Ops:
  0.6 0.7 %copy-start.9 = (f32[3,128]{1,0:T(4,128)S(1)}, f32[3,128]{1,0:T(4,128)}, u32[]{:S(2)}) copy-start(f32[3,128]{1,0:T(4,128)} %edge_b.1) | copy-start | bytes 4612
  1.3 0.7 %copy-start.8 = (s32[1,4,128]{2,1,0:T(4,128)S(1)}, s32[1,4,128]{2,1,0:T(4,128)}, u32[]{:S(2)}) copy-start(s32[1,4,128]{2,1,0:T(4,128)} %param.22) | copy-start | bytes 6148
  1.3 0.7 %copy-start.7 = (s32[1024]{0:T(1024)S(1)}, s32[1024]{0:T(1024)}, u32[]{:S(2)}) copy-start(s32[1024]{0:T(1024)} %param.21) | copy-start | bytes 12292
  1.3 0.7 %copy-start.6 = (s32[1024]{0:T(1024)S(1)}, s32[1024]{0:T(1024)}, u32[]{:S(2)}) copy-start(s32[1024]{0:T(1024)} %param.20) | copy-start | bytes 12292
  1.3 0.7 %copy-start.11 = (s32[1,4]{1,0:T(1,128)S(1)}, s32[1,4]{1,0:T(1,128)}, u32[]{:S(2)}) copy-start(s32[1,4]{1,0:T(1,128)} %send_len.1) | copy-start | bytes 52
  1.3 0.7 %copy-start.12 = (f32[128]{0:T(128)S(1)}, f32[128]{0:T(128)}, u32[]{:S(2)}) copy-start(f32[128]{0:T(128)} %param.27) | copy-start | bytes 1540
  2.0 1.0 %copy-start = (bf16[1024,128]{1,0:T(8,128)(2,1)S(1)}, bf16[1024,128]{1,0:T(8,128)(2,1)}, u32[]{:S(2)}) copy-start(bf16[1024,128]{1,0:T(8,128)(2,1)} %edge_lat.1) | copy-start | bytes 786436
  3.0 0.9 %copy-start.1 = (bf16[1024,128]{1,0:T(8,128)(2,1)S(1)}, bf16[1024,128]{1,0:T(8,128)(2,1)}, u32[]{:S(2)}) copy-start(bf16[1024,128]{1,0:T(8,128)(2,1)} %edge_cot.1) | copy-start | bytes 786436
  3.9 0.9 %copy-start.2 = (bf16[5,128,128]{2,1,0:T(8,128)(2,1)S(1)}, bf16[5,128,128]{2,1,0:T(8,128)(2,1)}, u32[]{:S(2)}) copy-start(bf16[5,128,128]{2,1,0:T(8,128)(2,1)} %edge_w.1) | copy-start | bytes 491524
  4.9 0.9 %copy-start.3 = (bf16[4,128,128]{2,1,0:T(8,128)(2,1)S(1)}, bf16[4,128,128]{2,1,0:T(8,128)(2,1)}, u32[]{:S(2)}) copy-start(bf16[4,128,128]{2,1,0:T(8,128)(2,1)} %node_w.1) | copy-start | bytes 393220
  5.8 0.8 %copy-start.4 = (bf16[128,128]{1,0:T(8,128)(2,1)S(1)}, bf16[128,128]{1,0:T(8,128)(2,1)}, u32[]{:S(2)}) copy-start(bf16[128,128]{1,0:T(8,128)(2,1)} %node_lat.1) | copy-start | bytes 98308
  6.5 0.8 %copy-start.5 = (bf16[128,128]{1,0:T(8,128)(2,1)S(1)}, bf16[128,128]{1,0:T(8,128)(2,1)}, u32[]{:S(2)}) copy-start(bf16[128,128]{1,0:T(8,128)(2,1)} %node_cot.1) | copy-start | bytes 98308
  7.3 0.7 %copy-start.10 = (f32[3,128]{1,0:T(4,128)S(1)}, f32[3,128]{1,0:T(4,128)}, u32[]{:S(2)}) copy-start(f32[3,128]{1,0:T(4,128)} %node_b.1) | copy-start | bytes 4612
  8.0 0.7 %copy-start.13 = (f32[128]{0:T(128)S(1)}, f32[128]{0:T(128)}, u32[]{:S(2)}) copy-start(f32[128]{0:T(128)} %param.28) | copy-start | bytes 1540
  8.6 0.7 %copy-start.14 = (f32[128]{0:T(128)S(1)}, f32[128]{0:T(128)}, u32[]{:S(2)}) copy-start(f32[128]{0:T(128)} %param.31) | copy-start | bytes 1540

commit v2 on v1

--- a/solution.py
+++ b/solution.py
@@ -13,6 +13,7 @@
 BF16 = jnp.bfloat16
 LANES = 128
 CHUNK = 256
+VMEM_BYTES = 63 * 1024 * 1024
 
 
 def nn(left, right):
@@ -60,6 +61,33 @@
 
 def kernel(
     sizes,
+    hbm_node_lat,
+    hbm_edge_lat,
+    hbm_node_cot,
+    hbm_edge_cot,
+    hbm_senders,
+    hbm_receivers,
+    hbm_send_idx,
+    hbm_send_len,
+    hbm_edge_count,
+    hbm_edge_w,
+    hbm_edge_b,
+    hbm_edge_g,
+    hbm_edge_s,
+    hbm_node_w,
+    hbm_node_b,
+    hbm_node_g,
+    hbm_out_nodes,
+    hbm_out_edges,
+    hbm_out_ew,
+    hbm_out_nw,
+    hbm_out_vec,
+    out_nodes,
+    out_edges,
+    out_ew,
+    out_nw,
+    out_vec,
+    store_sem,
     node_lat,
     edge_lat,
     node_cot,
@@ -76,12 +104,7 @@
     node_w,
     node_b,
     node_g,
-    out_nodes,
-    out_edges,
-    out_ew,
-    out_ev,
-    out_nw,
-    out_nv,
+    load_sem,
     ext,
     outgoing,
     oh_s,
@@ -154,6 +177,38 @@
     vz_s,
     vz_r,
 ):
+    loads = {}
+    for name, src, dst in (
+        ("node_lat", hbm_node_lat, node_lat),
+        ("edge_lat", hbm_edge_lat, edge_lat),
+        ("node_cot", hbm_node_cot, node_cot),
+        ("edge_cot", hbm_edge_cot, edge_cot),
+        ("senders", hbm_senders, senders),
+        ("receivers", hbm_receivers, receivers),
+        ("send_idx", hbm_send_idx, send_idx),
+        ("send_len", hbm_send_len, send_len),
+        ("edge_count", hbm_edge_count, edge_count),
+        ("edge_w", hbm_edge_w, edge_w),
+        ("edge_b", hbm_edge_b, edge_b),
+        ("edge_g", hbm_edge_g, edge_g),
+        ("edge_s", hbm_edge_s, edge_s),
+        ("node_w", hbm_node_w, node_w),
+        ("node_b", hbm_node_b, node_b),
+        ("node_g", hbm_node_g, node_g),
+    ):
+        loads[name] = pltpu.make_async_copy(src, dst, load_sem.at[len(loads)])
+        loads[name].start()
+
+    stores = []
+
+    def store(src, dst):
+        stores.append(pltpu.make_async_copy(src, dst, store_sem.at[len(stores)]))
+        stores[-1].start()
+
+    def ready(*wanted):
+        for name in wanted:
+            loads[name].wait()
+
     dom, n_edge, n_sub = sizes
     inner = n_edge * n_sub
     rows = node_lat.shape[0]
@@ -230,6 +285,7 @@
         )
     pl.semaphore_wait(barrier, inner - 1 + dom - 1)
 
+    ready("node_lat")
     gathered = inner_start(
         lambda target, o: node_lat, lambda mine, o: ext.at[part_slice(mine)], ag_s, ag_r
     )
@@ -238,6 +294,8 @@
     lane = lax.broadcasted_iota(jnp.int32, (LANES, LANES), 1)
     sublane = lax.broadcasted_iota(jnp.int32, (LANES, LANES), 0)
 
+    ready("send_idx", "send_len", "senders", "receivers")
+
     def columns_of(row):
         return jnp.transpose(jnp.broadcast_to(row, (LANES, LANES)))
 
@@ -245,7 +303,7 @@
         return jnp.where(mask, 1.0, 0.0).astype(BF16)
 
     for b in range(blocks):
-        row = jnp.where(lane[:1] < send_len[0, b], send_idx[b : b + 1, :], -1)
+        row = jnp.where(lane[:1] < send_len[:, b : b + 1], send_idx[b : b + 1, :], -1)
         column = columns_of(row)
         for t in range(0, part_rows, LANES):
             oh_i[b * slot : (b + 1) * slot, t : t + LANES] = hot(column == lane + t)
@@ -263,6 +321,10 @@
             oh_s[span, t : t + LANES] = hot(column_s == lane + t)
             oht_s[t : t + LANES, span] = hot(row_s == sublane + t)
 
+    ready(
+        "edge_lat", "edge_cot", "edge_count", "edge_w", "edge_b", "edge_g", "edge_s",
+        "node_cot", "node_w", "node_b", "node_g",
+    )
     arrive(gathered)
 
     outgoing[...] = nn(oh_i[...], ext[:part_rows, :]).astype(BF16)
@@ -316,7 +378,7 @@
         normed, inv_std = normalise(nn(act2, edge_w[4]) + edge_b[2:3, :])
         normed_e[span, :] = normed
         inv_e[span, :] = inv_std
-        valid = lax.broadcasted_iota(jnp.int32, (CHUNK, 1), 0) + c < edge_count[0, 0]
+        valid = lax.broadcasted_iota(jnp.int32, (CHUNK, 1), 0) + c < edge_count[...]
         low_y[span, :] = jnp.where(valid, normed * edge_g[...] + edge_s[...], 0.0).astype(BF16)
 
     own_acc[...] = nn(oht_r[...], low_y[...])
@@ -402,7 +464,7 @@
     sums = [jnp.zeros((1, LANES), F32) for _ in range(5)]
     for c in range(0, edges, CHUNK):
         span = slice(c, c + CHUNK)
-        valid = lax.broadcasted_iota(jnp.int32, (CHUNK, 1), 0) + c < edge_count[0, 0]
+        valid = lax.broadcasted_iota(jnp.int32, (CHUNK, 1), 0) + c < edge_count[...]
         cot = edge_cot[span, :].astype(F32)
         dy = jnp.where(valid, cot + nn(oh_r[span, :], agg[...]), 0.0)
         normed = normed_e[span, :]
@@ -419,6 +481,7 @@
         for position, term in enumerate((h1, h2, h3, dy * normed, dy)):
             sums[position] = sums[position] + column_sum(term)
 
+    store(out_edges, hbm_out_edges)
     for position in range(5):
         vec[position : position + 1, :] = sums[position]
     vec_in[me] = vec[...]
@@ -492,6 +555,7 @@
     for o in range(1, inner):
         mine = mine + own_recv[o].astype(F32)
     out_nodes[...] = out_nodes[...] + mine
+    store(out_nodes, hbm_out_nodes)
 
     arrive(edge_z)
     edge_ag = gather_start(ew_z, ew_fown, ew_full, eag_s, eag_r)
@@ -502,17 +566,68 @@
     vec_sum = vec_z[0]
     for d in range(1, dom):
         vec_sum = vec_sum + vec_z[d]
-    out_ev[...] = vec_sum[0:5, :] * edge_scale
-    out_nv[...] = vec_sum[8:12, :] * node_scale
+    out_vec[0:8, :] = vec_sum[0:8, :] * edge_scale
+    out_vec[8:16, :] = vec_sum[8:16, :] * node_scale
+    store(out_vec, hbm_out_vec)
     arrive(node_ag)
     out_nw[...] = nw_full[...].astype(F32) * node_scale
+    store(out_nw, hbm_out_nw)
     arrive(edge_ag)
     out_ew[...] = ew_full[...].astype(F32) * edge_scale
-
+    store(out_ew, hbm_out_ew)
+
+    for copy in stores:
+        copy.wait()
     for copy in pending:
         copy.wait_send()
     for copy, has_target, has_source in halo + returning:
         pl.when(has_target)(copy.wait_send)
+
+
+def store_kernel(
+    nodes,
+    edges,
+    ew,
+    nw,
+    vec,
+    out_nodes,
+    out_edges,
+    out_ew,
+    out_ev,
+    out_nw,
+    out_nv,
+    v_nodes,
+    v_edges,
+    v_ew,
+    v_nw,
+    v_ev,
+    v_nv,
+    load_sem,
+    store_sem,
+):
+    routes = (
+        (vec.at[0:5], v_ev, out_ev),
+        (vec.at[8:12], v_nv, out_nv),
+        (nodes, v_nodes, out_nodes),
+        (edges, v_edges, out_edges),
+        (nw, v_nw, out_nw),
+        (ew, v_ew, out_ew),
+    )
+    loads = [
+        pltpu.make_async_copy(src, mid, load_sem.at[position])
+        for position, (src, mid, _) in enumerate(routes)
+    ]
+    stores = [
+        pltpu.make_async_copy(mid, dst, store_sem.at[position])
+        for position, (_, mid, dst) in enumerate(routes)
+    ]
+    for copy in loads:
+        copy.start()
+    for load, copy in zip(loads, stores):
+        load.wait()
+        copy.start()
+    for copy in stores:
+        copy.wait()
 
 
 def local(sizes, *arrays):
@@ -560,9 +675,7 @@
         node_b,
         node_g.reshape(1, features),
     )
-    vmem = pl.BlockSpec(memory_space=pltpu.VMEM)
-    smem = pl.BlockSpec(memory_space=pltpu.SMEM)
-    in_specs = [smem if position in (7, 8) else vmem for position in range(len(operands))]
+    hbm = pl.BlockSpec(memory_space=pltpu.HBM)
 
     def low(*shape):
         return pltpu.VMEM(shape + (features,), BF16)
@@ -584,6 +697,14 @@
         return [pltpu.SemaphoreType.DMA((count,)), pltpu.SemaphoreType.DMA((count,))]
 
     scratch = [
+        full(rows),
+        low(edges),
+        full(5, features),
+        full(4, features),
+        full(16),
+        pltpu.SemaphoreType.DMA((5,)),
+        *[pltpu.VMEM(array.shape, array.dtype) for array in operands],
+        pltpu.SemaphoreType.DMA((len(operands),)),
         low(ext_rows),
         low(blocks * slot),
         pltpu.VMEM((edges, ext_rows), BF16),
@@ -632,8 +753,24 @@
         *sems(inner),
         *sems(dom),
     ]
+    results = pl.pallas_call(
+        functools.partial(kernel, sizes),
+        out_shape=(
+            jax.ShapeDtypeStruct((rows, features), F32),
+            jax.ShapeDtypeStruct((edges, features), BF16),
+            jax.ShapeDtypeStruct((5, features, features), F32),
+            jax.ShapeDtypeStruct((4, features, features), F32),
+            jax.ShapeDtypeStruct((16, features), F32),
+        ),
+        in_specs=[hbm] * len(operands),
+        out_specs=(hbm,) * 5,
+        scratch_shapes=scratch,
+        compiler_params=pltpu.CompilerParams(
+            collective_id=0, has_side_effects=True, vmem_limit_bytes=VMEM_BYTES
+        ),
+    )(*operands)
     return pl.pallas_call(
-        functools.partial(kernel, sizes),
+        store_kernel,
         out_shape=(
             jax.ShapeDtypeStruct((rows, features), F32),
             jax.ShapeDtypeStruct((edges, features), BF16),
@@ -642,13 +779,20 @@
             jax.ShapeDtypeStruct((4, features, features), F32),
             jax.ShapeDtypeStruct((4, features), F32),
         ),
-        in_specs=in_specs,
-        out_specs=(vmem,) * 6,
-        scratch_shapes=scratch,
-        compiler_params=pltpu.CompilerParams(
-            collective_id=0, has_side_effects=True, vmem_limit_bytes=48 * 1024 * 1024
-        ),
-    )(*operands)
+        in_specs=[hbm] * 5,
+        out_specs=(hbm,) * 6,
+        scratch_shapes=[
+            full(rows),
+            low(edges),
+            full(5, features),
+            full(4, features),
+            full(5),
+            full(4),
+            pltpu.SemaphoreType.DMA((6,)),
+            pltpu.SemaphoreType.DMA((6,)),
+        ],
+        compiler_params=pltpu.CompilerParams(vmem_limit_bytes=VMEM_BYTES),
+    )(*results)
 
 
 def solution(mesh):

time: 54.1 us -> 44.4 us (0.82)
  local copies, waits for them, and re-layouts: 11.8 us -> 0 us
  Pallas kernels: 40.4 us -> 42.9 us
    unnamed x36 -> x0, local copies, waits for them, and re-layouts: 11.8 us -> none
    pallas_call x0 -> x1, Pallas kernels: none -> 2.01 us  [local(): pl.pallas_call(store_kernel, out_shape=(jax.ShapeDtypeStruct((rows, featu...]
where the time goes in v2:
time: 44.4 us; the launch traced here: 44.2 us
  Pallas kernels  42.9 us (97%)
  between operations  1.29 us (3%)
    pallas_call x1, Pallas kernels, local(): pl.pallas_call(functools.partial(kernel, sizes), out_shape=(jax.ShapeDtyp...  40.9 us
    pallas_call x1, Pallas kernels, local(): pl.pallas_call(store_kernel, out_shape=(jax.ShapeDtypeStruct((rows, featu...  2.01 us

profile of v2, /device:TPU:0, one launch (start us, length us, event | category | flops | bytes accessed | tf_op | source)
XLA Modules:
  0.0 44.2 jit_solution(6152875428346140279)
XLA Ops:
  1.3 40.9 %shard_map.199 = (f32[128,128]{1,0:T(8,128)}, bf16[1024,128]{1,0:T(8,128)(2,1)}, f32[5,128,128]{2,1,0:T(8,128)}, f32[4,128,128]{2,1,0:T(8,128)}, f32[16,128]{1,0:T(8,128)}) custom-call(bf16[128,128]{1,0:T(8,128)(2,1)} %hbm_node_lat.1, bf16[1024,128]{1,0:T(8,128)(2,1)} %hbm_edge_lat.1, bf16[128,128]{1,0:T(8,128)(2,1)} %hbm_node_cot.1, ...), custom_call_target="tpu_custom_call" | custom-call | tf_op jit(solution)/shard_map/pallas_call | solution.py:756
  42.1 2.0 %shard_map.200 = (f32[128,128]{1,0:T(8,128)}, bf16[1024,128]{1,0:T(8,128)(2,1)}, f32[5,128,128]{2,1,0:T(8,128)}, f32[5,128]{1,0:T(8,128)}, f32[4,128,128]{2,1,0:T(8,128)}, /*index=5*/f32[4,128]{1,0:T(4,128)}) custom-call(f32[128,128]{1,0:T(8,128)} %get-tuple-element.11.nodes, bf16[1024,128]{1,0:T(8,128)(2,1)} %get-tuple-element.12.edges, ...), custom_call_target="tpu_custom_call" | custom-call | tf_op jit(solution)/shard_map/pallas_call | solution.py:772

commit v3 on v2

--- a/solution.py
+++ b/solution.py
@@ -138,12 +138,18 @@
     nw_z,
     nw_fown,
     nw_full,
-    ew_stage,
-    ew_recv,
-    ew_zown,
-    ew_z,
-    ew_fown,
-    ew_full,
+    ea_stage,
+    ea_recv,
+    ea_zown,
+    ea_z,
+    ea_fown,
+    ea_full,
+    eb_stage,
+    eb_recv,
+    eb_zown,
+    eb_z,
+    eb_fown,
+    eb_full,
     vec,
     vec_in,
     vec_zown,
@@ -166,12 +172,18 @@
     nz_r,
     nag_s,
     nag_r,
-    ers_s,
-    ers_r,
-    ez_s,
-    ez_r,
-    eag_s,
-    eag_r,
+    ars_s,
+    ars_r,
+    az_s,
+    az_r,
+    aag_s,
+    aag_r,
+    brs_s,
+    brs_r,
+    bz_s,
+    bz_r,
+    bag_s,
+    bag_r,
     vrs_s,
     vrs_r,
     vz_s,
@@ -467,6 +479,9 @@
         valid = lax.broadcasted_iota(jnp.int32, (CHUNK, 1), 0) + c < edge_count[...]
         cot = edge_cot[span, :].astype(F32)
         dy = jnp.where(valid, cot + nn(oh_r[span, :], agg[...]), 0.0)
+        if c == edges // CHUNK // 2 * CHUNK:
+            arrive(node_rs)
+            node_z = reduce_finish(nw_stage, nw_recv, nw_zown, nw_z, nz_s, nz_r)
         normed = normed_e[span, :]
         h3 = norm_backward(dy * edge_g[...], normed, inv_e[span, :])
         h3_low = h3.astype(BF16)
@@ -510,20 +525,21 @@
 
         returning.append((copy, has_target, has_source))
 
+    ea_stage[0] = tn(edge_lat[...], d1[...]).astype(BF16)
+    ea_stage[1] = tn(a1[...], d2[...]).astype(BF16)
+    ea_stage[2] = tn(a2[...], d3[...]).astype(BF16)
+    ea_rs = reduce_start(ea_stage, ea_recv, ars_s, ars_r)
     own_low = nn(oht_s[:part_rows, :], d1[...]).astype(BF16)
     recv_low = nn(oht_r[...], d1[...]).astype(BF16)
-    ew_stage[0] = tn(edge_lat[...], d1[...]).astype(BF16)
-    ew_stage[1] = (tn(ext[:part_rows, :], own_low) + tn(ext[part_rows:, :], back_send[...])).astype(
+    eb_stage[0] = (tn(ext[:part_rows, :], own_low) + tn(ext[part_rows:, :], back_send[...])).astype(
         BF16
     )
-    ew_stage[2] = tn(ext[:part_rows, :], recv_low).astype(BF16)
-    ew_stage[3] = tn(a1[...], d2[...]).astype(BF16)
-    ew_stage[4] = tn(a2[...], d3[...]).astype(BF16)
-    edge_rs = reduce_start(ew_stage, ew_recv, ers_s, ers_r)
+    eb_stage[1] = tn(ext[:part_rows, :], recv_low).astype(BF16)
+    eb_rs = reduce_start(eb_stage, eb_recv, brs_s, brs_r)
     own_acc[...] = nt(own_low, edge_w[1]) + nt(recv_low, edge_w[2])
 
-    arrive(node_rs)
-    node_z = reduce_finish(nw_stage, nw_recv, nw_zown, nw_z, nz_s, nz_r)
+    arrive(ea_rs)
+    ea_zs = reduce_finish(ea_stage, ea_recv, ea_zown, ea_z, az_s, az_r)
 
     for copy, has_target, has_source in returning:
         pl.when(has_source)(copy.wait_recv)
@@ -537,8 +553,8 @@
         own_r,
     )
 
-    arrive(edge_rs)
-    edge_z = reduce_finish(ew_stage, ew_recv, ew_zown, ew_z, ez_s, ez_r)
+    arrive(eb_rs)
+    eb_zs = reduce_finish(eb_stage, eb_recv, eb_zown, eb_z, bz_s, bz_r)
     arrive(vec_rs)
     vec_sum = vec_in[0]
     for position in range(1, inner):
@@ -550,15 +566,17 @@
     arrive(node_z)
     node_ag = gather_start(nw_z, nw_fown, nw_full, nag_s, nag_r)
 
+    arrive(ea_zs)
+    ea_ag = gather_start(ea_z, ea_fown, ea_full, aag_s, aag_r)
+    arrive(eb_zs)
+    eb_ag = gather_start(eb_z, eb_fown, eb_full, bag_s, bag_r)
+
     arrive(owning)
     mine = own_acc[part_slice(me), :]
     for o in range(1, inner):
         mine = mine + own_recv[o].astype(F32)
     out_nodes[...] = out_nodes[...] + mine
     store(out_nodes, hbm_out_nodes)
-
-    arrive(edge_z)
-    edge_ag = gather_start(ew_z, ew_fown, ew_full, eag_s, eag_r)
 
     edge_scale = 1.0 / math.sqrt(edges * dom * inner)
     node_scale = 1.0 / math.sqrt(rows * dom * inner)
@@ -572,8 +590,11 @@
     arrive(node_ag)
     out_nw[...] = nw_full[...].astype(F32) * node_scale
     store(out_nw, hbm_out_nw)
-    arrive(edge_ag)
-    out_ew[...] = ew_full[...].astype(F32) * edge_scale
+    arrive(ea_ag)
+    out_ew[0] = ea_full[0].astype(F32) * edge_scale
+    out_ew[3:5] = ea_full[1:3].astype(F32) * edge_scale
+    arrive(eb_ag)
+    out_ew[1:3] = eb_full[...].astype(F32) * edge_scale
     store(out_ew, hbm_out_ew)
 
     for copy in stores:
@@ -733,7 +754,8 @@
         low(part_rows),
         low(inner, rows),
         *weights(4),
-        *weights(5),
+        *weights(3),
+        *weights(2),
         full(16),
         full(inner, 16),
         full(16),
@@ -743,6 +765,9 @@
         *sems(inner),
         *sems(inner),
         *sems(blocks),
+        *sems(inner),
+        *sems(inner),
+        *sems(dom),
         *sems(inner),
         *sems(inner),
         *sems(dom),

time: 44.4 us -> 43.8 us (0.986)
  Pallas kernels: 42.9 us -> 42.4 us
    pallas_call x1, Pallas kernels: 40.9 us -> 40.4 us  [local(): pl.pallas_call(functools.partial(kernel, sizes), out_shape=(jax.ShapeDtyp...]
where the time goes in v3:
time: 43.8 us; the launch traced here: 43.7 us
  Pallas kernels  42.4 us (97%)
  between operations  1.29 us (3%)
    pallas_call x1, Pallas kernels, local(): pl.pallas_call(functools.partial(kernel, sizes), out_shape=(jax.ShapeDtyp...  40.4 us
    pallas_call x1, Pallas kernels, local(): pl.pallas_call(store_kernel, out_shape=(jax.ShapeDtypeStruct((rows, featu...  2.01 us

profile of v3, /device:TPU:0, one launch (start us, length us, event | category | flops | bytes accessed | tf_op | source)
XLA Modules:
  0.0 43.7 jit_solution(18046171724065948631)
XLA Ops:
  1.3 40.4 %shard_map.199 = (f32[128,128]{1,0:T(8,128)}, bf16[1024,128]{1,0:T(8,128)(2,1)}, f32[5,128,128]{2,1,0:T(8,128)}, f32[4,128,128]{2,1,0:T(8,128)}, f32[16,128]{1,0:T(8,128)}) custom-call(bf16[128,128]{1,0:T(8,128)(2,1)} %hbm_node_lat.1, bf16[1024,128]{1,0:T(8,128)(2,1)} %hbm_edge_lat.1, bf16[128,128]{1,0:T(8,128)(2,1)} %hbm_node_cot.1, ...), custom_call_target="tpu_custom_call" | custom-call | tf_op jit(solution)/shard_map/pallas_call | solution.py:781
  41.7 2.0 %shard_map.200 = (f32[128,128]{1,0:T(8,128)}, bf16[1024,128]{1,0:T(8,128)(2,1)}, f32[5,128,128]{2,1,0:T(8,128)}, f32[5,128]{1,0:T(8,128)}, f32[4,128,128]{2,1,0:T(8,128)}, /*index=5*/f32[4,128]{1,0:T(4,128)}) custom-call(f32[128,128]{1,0:T(8,128)} %get-tuple-element.11.nodes, bf16[1024,128]{1,0:T(8,128)(2,1)} %get-tuple-element.12.edges, ...), custom_call_target="tpu_custom_call" | custom-call | tf_op jit(solution)/shard_map/pallas_call | solution.py:797
